TPU v7x, 32 devices: a whole 2x2x4 slice. The times are simulated.
32 devices in a mesh: dp: 2 (over x), heads: 4 (over y, core), tensor: 4 (over z).
Axes of the slice: x: 2, y: 2, z: 4, core: 2. Of those that a mesh axis runs over, the one named last changes fastest.
Arguments:
- patches: bfloat16 [64, 196, 768], P(('dp', 'tensor')), may hold values from -6 to 6
- masked: int32 [64, 75], P(('dp', 'tensor')), may hold values from 0 to 195, as said below
- targets: int32 [64, 75], P('dp'), may hold values from 0 to 8191
- patch_weight: float32 [768, 768], P(('dp', 'heads', 'tensor')), may hold values from -0.21875 to 0.21875
- patch_first: float32 [768, 768], P(('dp', 'heads', 'tensor')), may hold values from -0.003125 to 0.003125
- patch_second: float32 [768, 768], P(('dp', 'heads', 'tensor')), may hold values from 1.0850695e-06 to 4.340278e-06
- attention_weight: float32 [2, 768, 3072], P(None, ('dp', 'tensor'), 'heads')
- attention_first: float32 [2, 768, 3072], P(None, ('dp', 'tensor'), 'heads'), may hold values from -0.003125 to 0.003125
- attention_second: float32 [2, 768, 3072], P(None, ('dp', 'tensor'), 'heads'), may hold values from 1.0850695e-06 to 4.340278e-06
- hidden_weight: float32 [2, 2, 768, 3072], P(None, None, ('dp', 'heads'), 'tensor'), may hold values from -0.21875 to 0.21875
- hidden_first: float32 [2, 2, 768, 3072], P(None, None, ('dp', 'heads'), 'tensor'), may hold values from -0.003125 to 0.003125
- hidden_second: float32 [2, 2, 768, 3072], P(None, None, ('dp', 'heads'), 'tensor'), may hold values from 1.0850695e-06 to 4.340278e-06
- head_weight: float32 [768, 8192], P(('dp', 'heads'), 'tensor'), may hold values from -0.4375 to 0.4375
- head_first: float32 [768, 8192], P(('dp', 'heads'), 'tensor'), may hold values from -0.00047841595 to 0.00047841595
- head_second: float32 [768, 8192], P(('dp', 'heads'), 'tensor'), may hold values from 2.5431316e-08 to 1.0172526e-07
- vector_table: float32 [16, 768], replicated
- vector_first: float32 [16, 768], replicated, may hold values from -0.003125 to 0.003125
- vector_second: float32 [16, 768], replicated, may hold values from 1.0850695e-06 to 4.340278e-06
- relative_bias: float32 [12, 732], replicated, may hold values from -3 to 3
- bias_first: float32 [12, 732], replicated, may hold values from -0.00015625 to 0.00015625
- bias_second: float32 [12, 732], replicated, may hold values from 2.7126736e-09 to 1.0850695e-08
Outputs:
- loss: float32 [], replicated
- updated_patch: float32 [768, 768], P(('dp', 'heads', 'tensor'))
- moment_patch: float32 [768, 768], P(('dp', 'heads', 'tensor'))
- square_patch: float32 [768, 768], P(('dp', 'heads', 'tensor'))
- updated_attention: float32 [2, 768, 3072], P(None, ('dp', 'tensor'), 'heads')
- moment_attention: float32 [2, 768, 3072], P(None, ('dp', 'tensor'), 'heads')
- square_attention: float32 [2, 768, 3072], P(None, ('dp', 'tensor'), 'heads')
- updated_hidden: float32 [2, 2, 768, 3072], P(None, None, ('dp', 'heads'), 'tensor')
- moment_hidden: float32 [2, 2, 768, 3072], P(None, None, ('dp', 'heads'), 'tensor')
- square_hidden: float32 [2, 2, 768, 3072], P(None, None, ('dp', 'heads'), 'tensor')
- updated_head: float32 [768, 8192], P(('dp', 'heads'), 'tensor')
- moment_head: float32 [768, 8192], P(('dp', 'heads'), 'tensor')
- square_head: float32 [768, 8192], P(('dp', 'heads'), 'tensor')
- updated_vectors: float32 [16, 768], replicated
- moment_vectors: float32 [16, 768], replicated
- square_vectors: float32 [16, 768], replicated
- updated_bias: float32 [12, 732], replicated
- moment_bias: float32 [12, 732], replicated
- square_bias: float32 [12, 732], replicated
Inputs may be any that keep to these rules, and one draw needn't show every extreme that they name: `masked`: the 75 entries of an image are different patch numbers.
All inputs are finite; a program needn't handle non-finite values.
Results may differ from a plain program's by a relative error of at most 0.015.
The roundings to bfloat16 on the way count: a program that leaves them out, or rounds other values in their place, can miss the bound.
Values may be sent and summed in bfloat16 or wider, within the bound.
No kernel may reach another device: no remote copies, remote signals or barrier semaphores. Data moves between devices by JAX's collectives and lax.ppermute only.
A program may use at most 256 MiB of HBM per device.

v0:
```python
from functools import partial

import jax
import jax.numpy as jnp
import numpy as np
from jax import lax
from jax.sharding import PartitionSpec as P

HEAD_DIM = 64
GRID = 14
STEP = 3


epsilon = 1e-06
beta_one = 0.5
beta_two = 0.5
adam_floor = 1e-08
decay_rate = 0.05
learning_rates = (0.03, 0.03, 0.02, 0.03, 0.3, 0.3)


def merged(part, axis, combine):
    gathered = jax.tree.map(lambda a: lax.all_gather(a, axis), part)

    def take(source):
        return jax.tree.map(lambda a: lax.dynamic_index_in_dim(a, source, 0, False), gathered)

    return lax.fori_loop(
        1, lax.axis_size(axis), lambda source, state: combine(state, take(source)), take(0)
    )


def relative_index(grid_side):
    coords = np.stack(
        np.meshgrid(np.arange(grid_side), np.arange(grid_side), indexing="ij")
    ).reshape(2, -1)
    delta = coords[:, :, None] - coords[:, None, :]
    inner = (delta[0] + grid_side - 1) * (2 * grid_side - 1) + delta[1] + grid_side - 1
    corner = (2 * grid_side - 1) ** 2
    index_table = np.zeros((grid_side * grid_side + 1, grid_side * grid_side + 1), np.int32)
    index_table[1:, 1:] = inner
    index_table[0, 1:] = corner
    index_table[1:, 0] = corner + 1
    index_table[0, 0] = corner + 2
    return index_table


def norm_rows(values, gain_row, shift_row):
    centred = values - jnp.mean(values, -1, keepdims=True)
    scaled = lax.rsqrt(jnp.mean(centred * centred, -1, keepdims=True) + epsilon)
    return centred * scaled * gain_row + shift_row


def rows_heads(values):
    return lax.all_gather(values, "heads", axis=0, tiled=True)


def sum_heads(values):
    return lax.psum_scatter(
        values.astype(jnp.bfloat16), "heads", scatter_dimension=0, tiled=True
    ).astype(jnp.float32)


def rows_tensor(values):
    return lax.all_gather(values, "tensor", axis=0, tiled=True)


def sum_tensor(values):
    return lax.psum_scatter(
        values.astype(jnp.bfloat16), "tensor", scatter_dimension=0, tiled=True
    ).astype(jnp.float32)


def fetch_layer(attention_weight, hidden_weight, layer_at):
    attention_full = lax.all_gather(
        attention_weight[layer_at].astype(jnp.bfloat16), ("dp", "tensor"), axis=0, tiled=True
    )
    hidden_full = lax.all_gather(
        hidden_weight[layer_at].astype(jnp.bfloat16), ("dp", "heads"), axis=1, tiled=True
    )
    return (attention_full, hidden_full)


def contract_rows(left_side, right_side):
    return lax.dot_general(
        left_side, right_side, (((0,), (0,)), ((), ())), preferred_element_type=jnp.float32
    )


def contract_columns(left_side, right_side):
    return lax.dot_general(
        left_side, right_side, (((1,), (1,)), ((), ())), preferred_element_type=jnp.float32
    )


def split_columns(attention_full):
    quarter_width = attention_full.shape[1] // 4
    return (attention_full[:, : 3 * quarter_width], attention_full[:, 3 * quarter_width :])


def attention_forward(gathered, project_weight, output_weight, bias_grid, images, head_width):
    tokens = gathered.shape[0] // images
    head_count = project_weight.shape[1] // (3 * head_width)
    projected = jnp.dot(gathered, project_weight, preferred_element_type=jnp.float32).reshape(
        images, tokens, head_count, 3, head_width
    )
    query_rows = (projected[:, :, :, 0] * head_width ** (-0.5)).astype(jnp.bfloat16)
    key_rows = projected[:, :, :, 1].astype(jnp.bfloat16)
    value_rows = projected[:, :, :, 2].astype(jnp.bfloat16)
    scores = (
        jnp.einsum("gqhe,gkhe->ghqk", query_rows, key_rows, preferred_element_type=jnp.float32)
        + bias_grid[None]
    )
    score_max = jnp.max(scores, -1, keepdims=True)
    score_lse = jnp.log(jnp.sum(jnp.exp(scores - score_max), -1, keepdims=True)) + score_max
    weights = jnp.exp(scores - score_lse).astype(jnp.bfloat16)
    context = jnp.einsum(
        "ghqk,gkhe->gqhe", weights, value_rows, preferred_element_type=jnp.float32
    ).astype(jnp.bfloat16)
    context = context.reshape(images * tokens, head_count * head_width)
    return (
        contract_columns(context, output_weight),
        (query_rows, key_rows, value_rows, score_lse, context),
    )


def attention_backward(
    gathered,
    attended_rows,
    project_weight,
    output_weight,
    saved_attention,
    bias_grid,
    images,
    head_width,
):
    query_rows, key_rows, value_rows, score_lse, context = saved_attention
    tokens = gathered.shape[0] // images
    head_count = query_rows.shape[2]
    grad_output = contract_rows(attended_rows, context)
    grad_context = jnp.dot(attended_rows, output_weight, preferred_element_type=jnp.float32).astype(
        jnp.bfloat16
    )
    grad_context = grad_context.reshape(images, tokens, head_count, head_width)
    scores = (
        jnp.einsum("gqhe,gkhe->ghqk", query_rows, key_rows, preferred_element_type=jnp.float32)
        + bias_grid[None]
    )
    weights = jnp.exp(scores - score_lse)
    grad_weights = jnp.einsum(
        "gqhe,gkhe->ghqk", grad_context, value_rows, preferred_element_type=jnp.float32
    )
    grad_value = jnp.einsum(
        "ghqk,gqhe->gkhe",
        weights.astype(jnp.bfloat16),
        grad_context,
        preferred_element_type=jnp.float32,
    )
    grad_scores = weights * (grad_weights - jnp.sum(weights * grad_weights, -1, keepdims=True))
    grad_bias = jnp.sum(grad_scores, 0)
    rounded = grad_scores.astype(jnp.bfloat16)
    grad_query = jnp.einsum(
        "ghqk,gkhe->gqhe", rounded, key_rows, preferred_element_type=jnp.float32
    ) * head_width ** (-0.5)
    grad_key = jnp.einsum(
        "ghqk,gqhe->gkhe", rounded, query_rows, preferred_element_type=jnp.float32
    )
    grad_projected = (
        jnp.stack([grad_query, grad_key, grad_value], 3)
        .astype(jnp.bfloat16)
        .reshape(images * tokens, -1)
    )
    grad_project = contract_rows(gathered, grad_projected)
    grad_gathered = contract_columns(grad_projected, project_weight)
    return (grad_project, grad_output, grad_gathered, grad_bias)


def adam_update(weight, first_moment, second_moment, gradient, rate):
    first_new = beta_one * first_moment + (1.0 - beta_one) * gradient
    second_new = beta_two * second_moment + (1.0 - beta_two) * gradient * gradient
    first_fix = 1.0 - beta_one**STEP
    second_fix = 1.0 - beta_two**STEP
    stepped = first_new / first_fix / (jnp.sqrt(second_new / second_fix) + adam_floor)
    return (weight - rate * (stepped + decay_rate * weight), first_new, second_new)


def combine(first_part, second_part):
    joint_max = jnp.maximum(first_part[0], second_part[0])
    joint_sum = first_part[1] * jnp.exp(first_part[0] - joint_max) + second_part[1] * jnp.exp(
        second_part[0] - joint_max
    )
    return (joint_max, joint_sum)


def shards(
    patches,
    masked,
    targets,
    patch_weight,
    patch_first,
    patch_second,
    attention_weight,
    attention_first,
    attention_second,
    hidden_weight,
    hidden_first,
    hidden_second,
    head_weight,
    head_first,
    head_second,
    vector_table,
    vector_first,
    vector_second,
    relative_bias,
    bias_first,
    bias_second,
):
    heads_index = lax.axis_index("heads")
    heads_size = lax.axis_size("heads")
    tensor_index = lax.axis_index("tensor")
    tensor_size = lax.axis_size("tensor")
    images = patches.shape[0]
    tokens = patches.shape[1] + 1
    marked = masked.shape[1]
    layer_count = attention_weight.shape[0]
    head_width = HEAD_DIM
    quarter = images * tokens // heads_size
    total_rows = images * marked * lax.axis_size("dp") * tensor_size
    index_table = jnp.asarray(relative_index(GRID))
    final_base = 6 * layer_count
    padded = jnp.concatenate(
        [jnp.zeros((images, 1, patches.shape[2]), jnp.bfloat16), patches], 1
    ).reshape(images * tokens, patches.shape[2])
    local_pixels = lax.dynamic_slice_in_dim(padded, heads_index * quarter, quarter)
    patch_full = lax.all_gather(
        patch_weight.astype(jnp.bfloat16), ("dp", "heads", "tensor"), axis=0, tiled=True
    )
    embedded = jnp.dot(local_pixels, patch_full, preferred_element_type=jnp.float32)
    mask_grid = jnp.any(
        masked[:, :, None] + 1 == jnp.arange(tokens)[None, None, :], axis=1
    ).reshape(-1)
    is_masked = lax.dynamic_slice_in_dim(mask_grid, heads_index * quarter, quarter)[:, None]
    is_class = ((heads_index * quarter + jnp.arange(quarter)) % tokens == 0)[:, None]
    residual = jnp.where(
        is_class,
        vector_table[final_base + 2],
        jnp.where(is_masked, vector_table[final_base + 3], embedded),
    )
    head_count = relative_bias.shape[0] // heads_size
    own_bias = lax.dynamic_slice_in_dim(relative_bias, heads_index * head_count, head_count)
    bias_grid = jnp.take(own_bias, index_table, axis=1)
    saved_layers = []
    for layer_at in range(layer_count):
        attention_full, hidden_full = fetch_layer(attention_weight, hidden_weight, layer_at)
        gain_rows = vector_table[6 * layer_at : 6 * layer_at + 6]
        normed = norm_rows(residual, gain_rows[0], gain_rows[1]).astype(jnp.bfloat16)
        gathered = rows_heads(normed)
        project_weight, output_weight = split_columns(attention_full)
        partial_sums, saved_attention = attention_forward(
            gathered, project_weight, output_weight, bias_grid, images, head_width
        )
        attended = sum_heads(partial_sums)
        middle = residual + gain_rows[2] * attended
        mixed_rows = norm_rows(middle, gain_rows[3], gain_rows[4]).astype(jnp.bfloat16)
        group_rows = rows_tensor(mixed_rows)
        hidden = jnp.dot(group_rows, hidden_full[0], preferred_element_type=jnp.float32)
        activated = jax.nn.gelu(hidden, approximate=False).astype(jnp.bfloat16)
        output = sum_tensor(contract_columns(activated, hidden_full[1]))
        weights_kept = None
        saved_layers.append(
            (
                residual,
                middle,
                gathered,
                saved_attention,
                attended,
                group_rows,
                hidden,
                activated,
                output,
                weights_kept,
            )
        )
        residual = middle + gain_rows[5] * output
    final_rows = norm_rows(residual, vector_table[final_base], vector_table[final_base + 1]).astype(
        jnp.bfloat16
    )
    final_all = rows_heads(final_rows)
    row_index = (jnp.arange(images)[:, None] * tokens + masked + 1).reshape(-1)
    share_rows = images * marked // heads_size
    own_index = lax.dynamic_slice_in_dim(row_index, heads_index * share_rows, share_rows)
    picked = jnp.take(final_all, own_index, axis=0)
    head_rows = rows_tensor(picked)
    head_full = lax.all_gather(
        head_weight.astype(jnp.bfloat16), ("dp", "heads"), axis=0, tiled=True
    )
    logits = jnp.dot(head_rows, head_full, preferred_element_type=jnp.float32)
    block_width = logits.shape[1]
    target_rows = targets.reshape(tensor_size, images * marked)
    target_rows = lax.dynamic_slice_in_dim(
        target_rows, heads_index * share_rows, share_rows, 1
    ).reshape(-1)
    onehot = jnp.arange(block_width)[None, :] + tensor_index * block_width == target_rows[:, None]
    local_max = jnp.max(logits, -1)
    local_sum = jnp.sum(jnp.exp(logits - local_max[:, None]), -1)
    local_pick = jnp.sum(jnp.where(onehot, logits, 0.0), -1)
    score_max, score_sum = merged((local_max, local_sum), "tensor", combine)
    log_total = score_max + jnp.log(score_sum)
    loss_part = jnp.where(tensor_index == 0, jnp.sum(log_total), 0.0) - jnp.sum(local_pick)
    grad_logits = (
        (jnp.exp(logits - log_total[:, None]) - onehot.astype(jnp.float32)) / total_rows
    ).astype(jnp.bfloat16)
    head_grad = lax.psum_scatter(
        contract_rows(head_rows, grad_logits), ("dp", "heads"), scatter_dimension=0, tiled=True
    )
    grad_picked = sum_tensor(contract_columns(grad_logits, head_full))
    grad_all = (
        jnp.zeros((images * tokens, grad_picked.shape[1]), jnp.float32)
        .at[own_index]
        .add(grad_picked)
    )
    grad_final = sum_heads(grad_all)
    _, norm_back = jax.vjp(
        norm_rows, residual, vector_table[final_base], vector_table[final_base + 1]
    )
    grad_residual, grad_final_gain, grad_final_shift = norm_back(grad_final)
    bias_grad = jnp.zeros(bias_grid.shape, jnp.float32)
    layer_grads = [None] * layer_count
    attention_grads = [None] * layer_count
    hidden_grads = [None] * layer_count
    for layer_at in reversed(range(layer_count)):
        (
            residual_in,
            middle,
            gathered,
            saved_attention,
            attended,
            group_rows,
            hidden,
            activated,
            output,
            weights_kept,
        ) = saved_layers[layer_at]
        attention_full, hidden_full = fetch_layer(attention_weight, hidden_weight, layer_at)
        gain_rows = vector_table[6 * layer_at : 6 * layer_at + 6]
        grad_rows = [None] * 6
        grad_rows[5] = jnp.sum(grad_residual * output, 0)
        grad_output = (grad_residual * gain_rows[5]).astype(jnp.bfloat16)
        output_rows = rows_tensor(grad_output)
        grad_activated = jnp.dot(output_rows, hidden_full[1], preferred_element_type=jnp.float32)
        grad_down = contract_rows(output_rows, activated)
        _, gelu_back = jax.vjp(partial(jax.nn.gelu, approximate=False), hidden)
        grad_hidden = gelu_back(grad_activated)[0].astype(jnp.bfloat16)
        grad_up = contract_rows(group_rows, grad_hidden)
        grad_mixed = sum_tensor(contract_columns(grad_hidden, hidden_full[0]))
        _, norm_back = jax.vjp(norm_rows, middle, gain_rows[3], gain_rows[4])
        grad_middle, grad_rows[3], grad_rows[4] = norm_back(grad_mixed)
        grad_middle = grad_middle + grad_residual
        grad_rows[2] = jnp.sum(grad_middle * attended, 0)
        grad_attended = (grad_middle * gain_rows[2]).astype(jnp.bfloat16)
        attended_rows = rows_heads(grad_attended)
        project_weight, output_weight = split_columns(attention_full)
        grad_project, grad_output_weight, grad_gathered, grad_bias = attention_backward(
            gathered,
            attended_rows,
            project_weight,
            output_weight,
            saved_attention,
            bias_grid,
            images,
            head_width,
        )
        grad_normed = sum_heads(grad_gathered)
        _, norm_back = jax.vjp(norm_rows, residual_in, gain_rows[0], gain_rows[1])
        grad_input, grad_rows[0], grad_rows[1] = norm_back(grad_normed)
        grad_residual = grad_input + grad_middle
        bias_grad = bias_grad + grad_bias
        layer_grads[layer_at] = jnp.stack(grad_rows)
        attention_grads[layer_at] = lax.psum_scatter(
            jnp.concatenate([grad_project, grad_output_weight], 1),
            ("dp", "tensor"),
            scatter_dimension=0,
            tiled=True,
        )
        hidden_grads[layer_at] = lax.psum_scatter(
            jnp.stack([grad_up, grad_down]), ("dp", "heads"), scatter_dimension=1, tiled=True
        )
    grad_embedded = jnp.where(is_class | is_masked, 0.0, grad_residual).astype(jnp.bfloat16)
    patch_grad = lax.psum_scatter(
        contract_rows(local_pixels, grad_embedded),
        ("dp", "heads", "tensor"),
        scatter_dimension=0,
        tiled=True,
    )
    grad_class = jnp.sum(jnp.where(is_class, grad_residual, 0.0), 0)
    grad_mask = jnp.sum(jnp.where(is_masked, grad_residual, 0.0), 0)
    vector_grad = jnp.concatenate(
        layer_grads + [jnp.stack([grad_final_gain, grad_final_shift, grad_class, grad_mask])], 0
    )
    rel_count = relative_bias.shape[1]
    local_rel = jax.ops.segment_sum(
        bias_grad.reshape(head_count, -1).T, index_table.reshape(-1), rel_count
    ).T
    full_rel = lax.dynamic_update_slice_in_dim(
        jnp.zeros(relative_bias.shape, jnp.float32), local_rel, heads_index * head_count, 0
    )
    loss_total, vector_grad, relative_grad = lax.psum(
        (loss_part, vector_grad, full_rel), ("dp", "heads", "tensor")
    )
    loss = loss_total / total_rows
    params = (
        patch_weight,
        attention_weight,
        hidden_weight,
        head_weight,
        vector_table,
        relative_bias,
    )
    firsts = (patch_first, attention_first, hidden_first, head_first, vector_first, bias_first)
    seconds = (
        patch_second,
        attention_second,
        hidden_second,
        head_second,
        vector_second,
        bias_second,
    )
    gradients = (
        patch_grad,
        jnp.stack(attention_grads),
        jnp.stack(hidden_grads),
        head_grad,
        vector_grad,
        relative_grad,
    )
    results = [loss]
    for member in range(6):
        results.extend(
            adam_update(
                params[member],
                firsts[member],
                seconds[member],
                gradients[member],
                learning_rates[member],
            )
        )
    return tuple(results)


def solution(mesh):
    return jax.shard_map(
        shards,
        mesh=mesh,
        in_specs=(
            P(("dp", "tensor"), None, None),
            P(("dp", "tensor"), None),
            P("dp", None),
            P(("dp", "heads", "tensor"), None),
            P(("dp", "heads", "tensor"), None),
            P(("dp", "heads", "tensor"), None),
            P(None, ("dp", "tensor"), "heads"),
            P(None, ("dp", "tensor"), "heads"),
            P(None, ("dp", "tensor"), "heads"),
            P(None, None, ("dp", "heads"), "tensor"),
            P(None, None, ("dp", "heads"), "tensor"),
            P(None, None, ("dp", "heads"), "tensor"),
            P(("dp", "heads"), "tensor"),
            P(("dp", "heads"), "tensor"),
            P(("dp", "heads"), "tensor"),
            P(),
            P(),
            P(),
            P(),
            P(),
            P(),
        ),
        out_specs=(
            P(),
            P(("dp", "heads", "tensor"), None),
            P(("dp", "heads", "tensor"), None),
            P(("dp", "heads", "tensor"), None),
            P(None, ("dp", "tensor"), "heads"),
            P(None, ("dp", "tensor"), "heads"),
            P(None, ("dp", "tensor"), "heads"),
            P(None, None, ("dp", "heads"), "tensor"),
            P(None, None, ("dp", "heads"), "tensor"),
            P(None, None, ("dp", "heads"), "tensor"),
            P(("dp", "heads"), "tensor"),
            P(("dp", "heads"), "tensor"),
            P(("dp", "heads"), "tensor"),
            P(),
            P(),
            P(),
            P(),
            P(),
            P(),
        ),
        check_vma=False,
    )
```

profile of v0, /device:TPU:0, one launch (start us, length us, event | category | flops | bytes accessed | tf_op | source)
XLA Modules:
  0.0 1765.5 jit_solution(2604971572547548588)
XLA Ops:
  16.8 51.5 %all-gather.32.cloned.1.call-done = bf16[768,768]{1,0:T(8,128)(2,1)} async-done(((bf16[24,768]{1,0:T(8,128)(2,1)}), bf16[768,768]{1,0:T(8,128)(2,1)}) %all-gather.32.cloned.1.call-update) | async-done | bytes 1179664 | tf_op jit(solution)/shard_map/all_gather | solution.py:235
  74.1 128.5 %gather_fusion = f32[38809,3]{1,0:T(8,128)} fusion(f32[3,732]{0,1:T(8,128)S(1)} %copy.209, s32[38912]{0:T(1024)S(1)} %pad_clamp_fusion), kind=kCustom, calls=%fused_computation | custom fusion | bytes 1086652 | tf_op jit(solution)/shard_map/jit(_take)/gather | solution.py:251
  246.7 26.7 %fusion = bf16[400,768]{1,0:T(8,128)(2,1)S(1)} fusion(bf16[1576,768]{1,0:T(8,128)(2,1)} %convolution_convert_fusion.7), kind=kCustom, calls=%all-reduce-scatter | all-reduce-scatter fusion | flops 1228801 | bytes 3035648
  284.5 52.4 %all-gather.46.cloned.1.call-done = bf16[4,394,768]{2,1,0:T(8,128)(2,1)} async-done(((bf16[1,394,768]{2,1,0:T(8,128)(2,1)}), bf16[4,394,768]{2,1,0:T(8,128)(2,1)}) %all-gather.46.cloned.1.call-update) | async-done | bytes 2420752 | tf_op jit(solution)/shard_map/all_gather | solution.py:65
  340.7 26.4 %all-gather.38.cloned.1.call-done = bf16[1,2,768,768]{3,2,1,0:T(8,128)(2,1)} async-done(((bf16[1,2,96,768]{3,2,1,0:T(8,128)(2,1)}), bf16[1,2,768,768]{3,2,1,0:T(8,128)(2,1)}) %all-gather.38.cloned.1.call-update) | async-done | bytes 2359312 | tf_op jit(solution)/shard_map/all_gather | solution.py:78
  387.6 49.7 %fusion.1 = bf16[400,768]{1,0:T(8,128)(2,1)S(1)} fusion(bf16[1576,768]{1,0:T(8,128)(2,1)} %convolution_convert_fusion.6), kind=kCustom, calls=%all-reduce-scatter.1 | all-reduce-scatter fusion | flops 1228801 | bytes 3035648
  446.7 23.1 %all-gather.48.cloned.1.call-done = bf16[4,394,768]{2,1,0:T(8,128)(2,1)} async-done(((bf16[1,394,768]{2,1,0:T(8,128)(2,1)}), bf16[4,394,768]{2,1,0:T(8,128)(2,1)}) %all-gather.48.cloned.1.call-update) | async-done | bytes 2420752 | tf_op jit(solution)/shard_map/all_gather | solution.py:55
  472.2 41.4 %all-gather.40.cloned.1.call-done = bf16[1,768,768]{2,1,0:T(8,128)(2,1)} async-done(((bf16[1,96,768]{2,1,0:T(8,128)(2,1)}), bf16[1,768,768]{2,1,0:T(8,128)(2,1)}) %all-gather.40.cloned.1.call-update) | async-done | bytes 1179664 | tf_op jit(solution)/shard_map/all_gather | solution.py:75
  542.4 25.6 %fusion.2 = bf16[400,768]{1,0:T(8,128)(2,1)S(1)} fusion(bf16[1576,768]{1,0:T(8,128)(2,1)} %convolution_convert_fusion.5), kind=kCustom, calls=%all-reduce-scatter.2 | all-reduce-scatter fusion | flops 1228801 | bytes 3035648
  578.0 53.4 %all-gather.50.cloned.1.call-done = bf16[4,394,768]{2,1,0:T(8,128)(2,1)} async-done(((bf16[1,394,768]{2,1,0:T(8,128)(2,1)}), bf16[4,394,768]{2,1,0:T(8,128)(2,1)}) %all-gather.50.cloned.1.call-update) | async-done | bytes 2420752 | tf_op jit(solution)/shard_map/all_gather | solution.py:65
  635.1 26.6 %all-gather.42.cloned.1.call-done = bf16[1,2,768,768]{3,2,1,0:T(8,128)(2,1)} async-done(((bf16[1,2,96,768]{3,2,1,0:T(8,128)(2,1)}), bf16[1,2,768,768]{3,2,1,0:T(8,128)(2,1)}) %all-gather.42.cloned.1.call-update) | async-done | bytes 2359312 | tf_op jit(solution)/shard_map/all_gather | solution.py:78
  682.1 50.4 %fusion.3 = bf16[400,768]{1,0:T(8,128)(2,1)} fusion(bf16[1576,768]{1,0:T(8,128)(2,1)} %convolution_convert_fusion.4), kind=kCustom, calls=%all-reduce-scatter.3 | all-reduce-scatter fusion | flops 1228801 | bytes 3035648
  775.7 21.7 %all-gather.11 = bf16[4,150,768]{2,1,0:T(8,128)(2,1)} all-gather(bf16[1,150,768]{2,1,0:T(8,128)(2,1)S(1)} %select_bitcast_fusion), channel_id=1, replica_groups=mesh['dp'=2,'heads'=4,'tensor'=4] {'tensor'}, dimensions={0}, use_global_device_ids=true | all-gather | bytes 1152000 | tf_op jit(solution)/shard_map/all_gather | solution.py:65
  875.4 26.3 %fusion.5 = bf16[400,768]{1,0:T(8,128)(2,1)} fusion(bf16[1576,768]{1,0:T(8,128)(2,1)} %convert_element_type.243), kind=kCustom, calls=%all-reduce-scatter.5 | all-reduce-scatter fusion | flops 1228801 | bytes 3035648
  916.3 54.4 %all-gather.54.cloned.1.call-done = bf16[4,394,768]{2,1,0:T(8,128)(2,1)} async-done(((bf16[1,394,768]{2,1,0:T(8,128)(2,1)}), bf16[4,394,768]{2,1,0:T(8,128)(2,1)}) %all-gather.54.cloned.1.call-update) | async-done | bytes 2420752 | tf_op jit(solution)/shard_map/all_gather | solution.py:65
  987.7 48.3 %fusion.6 = bf16[400,768]{1,0:T(8,128)(2,1)} fusion(bf16[1576,768]{1,0:T(8,128)(2,1)} %convolution_convert_fusion.3), kind=kCustom, calls=%all-reduce-scatter.6 | all-reduce-scatter fusion | flops 1228801 | bytes 3035648
  1052.0 24.7 %all-gather.56.cloned.1.call-done = bf16[4,394,768]{2,1,0:T(8,128)(2,1)} async-done(((bf16[1,394,768]{2,1,0:T(8,128)(2,1)}), bf16[4,394,768]{2,1,0:T(8,128)(2,1)}) %all-gather.56.cloned.1.call-update) | async-done | bytes 2420752 | tf_op jit(solution)/shard_map/all_gather | solution.py:55
  1111.6 25.8 %fusion.7 = bf16[400,768]{1,0:T(8,128)(2,1)S(1)} fusion(bf16[1576,768]{1,0:T(8,128)(2,1)} %convolution_convert_fusion.2), kind=kCustom, calls=%all-reduce-scatter.7 | all-reduce-scatter fusion | flops 1228801 | bytes 3035648
  1151.9 56.4 %all-gather.58.cloned.1.call-done = bf16[4,394,768]{2,1,0:T(8,128)(2,1)} async-done(((bf16[1,394,768]{2,1,0:T(8,128)(2,1)}), bf16[4,394,768]{2,1,0:T(8,128)(2,1)}) %all-gather.58.cloned.1.call-update) | async-done | bytes 2420752 | tf_op jit(solution)/shard_map/all_gather | solution.py:65
  1222.5 47.6 %fusion.8 = bf16[400,768]{1,0:T(8,128)(2,1)S(1)} fusion(bf16[1576,768]{1,0:T(8,128)(2,1)} %convolution_convert_fusion.1), kind=kCustom, calls=%all-reduce-scatter.8 | all-reduce-scatter fusion | flops 1228801 | bytes 3035648
  1343.1 36.5 %fusion.9 = bf16[400,768]{1,0:T(8,128)(2,1)S(1)} fusion(bf16[1576,768]{1,0:T(8,128)(2,1)} %convolution_convert_fusion), kind=kCustom, calls=%all-reduce-scatter.9 | all-reduce-scatter fusion | flops 1228801 | bytes 3035648
  1445.2 207.7 %scatter_custom_fusion.1 = f32[732,3]{1,0:T(8,128)S(1)} fusion(s32[38809]{0:T(1024)} %constant.284, f32[38809,3]{1,0:T(8,128)} %copy.195, f32[]{:T(128)} %constant.123.clone.1), kind=kCustom, calls=%fused_computation.251 | custom fusion | flops 116427 | bytes 9296 | tf_op jit(solution)/shard_map/scatter-add | solution.py:401
  1657.0 44.4 %all-reduce.26 = (f32[]{:T(128)}, f32[16,768]{1,0:T(8,128)S(1)}, f32[12,732]{1,0:T(8,128)S(1)}) all-reduce(f32[]{:T(128)S(6)} %sub.196, f32[16,768]{1,0:T(8,128)S(1)} %concatenate.15, f32[12,732]{1,0:T(8,128)S(1)} %dynamic_update_slice.3), channel_id=1, replica_groups=mesh['dp'=2,'heads'=4,'tensor'=4] {'dp','heads','tensor'}, use_global_device_ids=true, to_apply=%region_25.26 | all-reduce | flops 21073 | bytes 168584 | tf_op jit(solution)/shard_map/psum | solution.py:407
  1709.6 45.1 %reduce-scatter.39.cloned.1.call-done = f32[96,768]{1,0:T(8,128)} async-done(((f32[768,768]{1,0:T(8,128)}), f32[96,768]{1,0:T(8,128)}) %reduce-scatter.39.cloned.1.call-update) | async-done | bytes 294928 | tf_op jit(solution)/shard_map/reduce_scatter | solution.py:379
  (611 shorter events, 548.6 us)
Async XLA Ops:
  7.2 61.2 %all-gather.32.cloned.1.call-start = ((), (), s32[]{:S(2)}) async-start(), calls=%async_computation.6 | async-start | bytes 1216512 | tf_op jit(solution)/shard_map/all_gather | solution.py:235
  8.8 205.8 %all-gather.44.cloned.1.call-start = ((), (), s32[]{:S(2)}) async-start(), calls=%async_computation.16 | async-start | bytes 3072000 | tf_op jit(solution)/shard_map/all_gather | solution.py:55
  72.1 146.3 %all-gather.36.cloned.1.call-start = ((), (), s32[]{:S(2)}) async-start(), calls=%async_computation.12 | async-start | bytes 1327104 | tf_op jit(solution)/shard_map/all_gather | solution.py:75
  73.0 264.0 %all-gather.46.cloned.1.call-start = ((), (), s32[]{:S(2)}) async-start(), calls=%async_computation.17 | async-start | bytes 3072000 | tf_op jit(solution)/shard_map/all_gather | solution.py:65
  283.1 84.1 %all-gather.38.cloned.1.call-start = ((), (), s32[]{:S(2)}) async-start(), calls=%async_computation.13 | async-start | bytes 2654208 | tf_op jit(solution)/shard_map/all_gather | solution.py:78
  284.5 185.3 %all-gather.48.cloned.1.call-start = ((), (), s32[]{:S(2)}) async-start(), calls=%async_computation.18 | async-start | bytes 3072000 | tf_op jit(solution)/shard_map/all_gather | solution.py:55
  445.9 67.7 %all-gather.40.cloned.1.call-start = ((), (), s32[]{:S(2)}) async-start(), calls=%async_computation.14 | async-start | bytes 1327104 | tf_op jit(solution)/shard_map/all_gather | solution.py:75
  446.7 184.7 %all-gather.50.cloned.1.call-start = ((), (), s32[]{:S(2)}) async-start(), calls=%async_computation.19 | async-start | bytes 3072000 | tf_op jit(solution)/shard_map/all_gather | solution.py:65
  577.2 84.5 %all-gather.42.cloned.1.call-start = ((), (), s32[]{:S(2)}) async-start(), calls=%async_computation.15 | async-start | bytes 2654208 | tf_op jit(solution)/shard_map/all_gather | solution.py:78
  577.9 190.8 %all-gather.52.cloned.1.call-start = ((), (), s32[]{:S(2)}) async-start(), calls=%async_computation.20 | async-start | bytes 3072000 | tf_op jit(solution)/shard_map/all_gather | solution.py:55
  744.8 58.8 %all-gather.34.cloned.1.call-start = ((), (), s32[]{:S(2)}) async-start(), calls=%async_computation.7 | async-start | bytes 3538944 | tf_op jit(solution)/shard_map/all_gather | solution.py:294
  746.8 223.9 %all-gather.54.cloned.1.call-start = ((), (), s32[]{:S(2)}) async-start(), calls=%async_computation.21 | async-start | bytes 3072000 | tf_op jit(solution)/shard_map/all_gather | solution.py:65
  862.9 3.1 collective-permute-start.4
  915.9 160.8 %all-gather.56.cloned.1.call-start = ((), (), s32[]{:S(2)}) async-start(), calls=%async_computation.22 | async-start | bytes 3072000 | tf_op jit(solution)/shard_map/all_gather | solution.py:55
  1036.8 3.5 collective-permute-start.6
  1051.8 156.5 %all-gather.58.cloned.1.call-start = ((), (), s32[]{:S(2)}) async-start(), calls=%async_computation.23 | async-start | bytes 3072000 | tf_op jit(solution)/shard_map/all_gather | solution.py:65
  1151.8 153.4 %all-gather.60.cloned.1.call-start = ((), (), s32[]{:S(2)}) async-start(), calls=%async_computation.24 | async-start | bytes 3072000 | tf_op jit(solution)/shard_map/all_gather | solution.py:55
  1270.1 3.5 collective-permute-start.8
  1280.3 373.3 %reduce-scatter.37.cloned.1.call-start = ((), (), s32[]{:S(2)}) async-start(), calls=%async_computation.11 | async-start | bytes 7077888 | tf_op jit(solution)/shard_map/reduce_scatter | solution.py:313
  1288.8 414.6 %reduce-scatter.31.cloned.1.call-start = ((), (), s32[]{:S(2)}) async-start(), calls=%async_computation.8 | async-start | bytes 2433024 | tf_op jit(solution)/shard_map/reduce_scatter | solution.py:389
  1394.1 310.9 %reduce-scatter.35.cloned.1.call-start = ((), (), s32[]{:S(2)}) async-start(), calls=%async_computation.10 | async-start | bytes 5308416 | tf_op jit(solution)/shard_map/reduce_scatter | solution.py:385
  1404.2 300.8 %reduce-scatter.33.cloned.1.call-start = ((), (), s32[]{:S(2)}) async-start(), calls=%async_computation.9 | async-start | bytes 5308416 | tf_op jit(solution)/shard_map/reduce_scatter | solution.py:385
  1414.8 294.8 %reduce-scatter.41.cloned.1.call-start = ((), (), s32[]{:S(2)}) async-start(), calls=%async_computation.26 | async-start | bytes 2654208 | tf_op jit(solution)/shard_map/reduce_scatter | solution.py:379
  1425.7 329.0 %reduce-scatter.39.cloned.1.call-start = ((), (), s32[]{:S(2)}) async-start(), calls=%async_computation.25 | async-start | bytes 2654208 | tf_op jit(solution)/shard_map/reduce_scatter | solution.py:379
  (157 other events, 5856.5 us)
Sparse Core Ops, SparseCore 0:
  11.5 56.8 all-gather.31
  72.2 23.5 all-gather.43
  98.5 41.0 all-gather.35
  283.2 53.7 all-gather.45
  339.3 27.7 all-gather.37
  446.0 23.7 all-gather.47
  472.5 41.0 all-gather.39
  577.3 53.9 all-gather.49
  633.8 27.7 all-gather.41
  744.9 23.7 all-gather.51
  771.2 32.3 all-gather.33
  916.0 54.6 all-gather.53
  1051.9 24.7 all-gather.55
  1152.0 56.2 all-gather.57
  1280.4 24.7 all-gather.59
  1308.5 69.1 reduce-scatter.36
  1394.2 102.1 reduce-scatter.30
  1499.7 52.8 reduce-scatter.34
  1556.5 53.8 reduce-scatter.32
  1613.7 69.2 reduce-scatter.40
  1686.5 68.1 reduce-scatter.38
where the time goes:
time: 1780 us; the launch traced here: 1770 us
  waiting for transfers between devices  507 us (28%)
  blocking collectives  441 us (25%)
  local copies, waits for them, and re-layouts  315 us (18%)
  other arithmetic  292 us (16%)
  matrix products  170 us (10%)
  between operations  22.6 us (1%)
    unnamed x11, blocking collectives  375 us
    all_gather x4, waiting for transfers between devices, rows_tensor(): return lax.all_gather(values, 'tensor', axis=0, tiled=True)  217 us
    scatter-add x1, other arithmetic, shards(): jax.ops.segment_sum(bias_grad.reshape(head_count, -1).T, index_table.resh...  208 us
    gather x4, local copies, waits for them, and re-layouts, shards(): bias_grid = jnp.take(own_bias, index_table, axis=1)  140 us
    unnamed x340, local copies, waits for them, and re-layouts  105 us
    all_gather x5, waiting for transfers between devices, rows_heads(): return lax.all_gather(values, 'heads', axis=0, tiled=True)  85 us
    all_gather x2, waiting for transfers between devices, fetch_layer(): lax.all_gather(hidden_weight[layer_at].astype(jnp.bfloat16), ('dp', 'head...  53 us
    all_gather x1, waiting for transfers between devices, shards(): lax.all_gather(patch_weight.astype(jnp.bfloat16), ('dp', 'heads', 'tensor...  51.5 us
  transfers between devices with their start and end apart: 31, of which 23 were waited for; matrix products, arithmetic and copies ran while one was open for 30% of the time, Pallas kernels for 0%

commit v1 on v0

v1 whole, which is shorter than its diff:
```python
from functools import partial

import jax
import jax.numpy as jnp
import numpy as np
from jax import lax
from jax.experimental import pallas as pl
from jax.experimental.pallas import tpu as pltpu
from jax.sharding import PartitionSpec as P

HEAD_DIM = 64
GRID = 14
STEP = 3
CORES = 2

epsilon = 1e-06
beta_one = 0.5
beta_two = 0.5
adam_floor = 1e-08
decay_rate = 0.05
learning_rates = (0.03, 0.03, 0.02, 0.03, 0.3, 0.3)
highest = lax.Precision.HIGHEST
ANY = pl.BlockSpec(memory_space=pl.ANY)
SMEM = pl.BlockSpec(memory_space=pltpu.SMEM)


class Place:
    def __init__(self):
        heads = lax.axis_size("heads")
        self.short = lax.axis_size("dp") <= 2
        self.size = {
            "x": lax.axis_size("dp"),
            "y": heads // CORES,
            "c": CORES,
            "z": lax.axis_size("tensor"),
        }
        head_at = lax.axis_index("heads")
        self.at = {
            "x": lax.axis_index("dp"),
            "y": head_at // CORES,
            "c": head_at % CORES,
            "z": lax.axis_index("tensor"),
        }
        self.scalars = jnp.stack([self.at[k] for k in "xycz"]).astype(jnp.int32)

    def hop(self, value, way):
        count = self.size[way]
        if way in "xz":
            axis = "dp" if way == "x" else "tensor"
            return lax.ppermute(value, axis, [(i, (i + 1) % count) for i in range(count)])
        if way == "y":
            pairs = [
                (i * CORES + c, (i + 1) % count * CORES + c)
                for i in range(count)
                for c in range(CORES)
            ]
        else:
            pairs = [
                (i * CORES + c, i * CORES + (c + 1) % CORES)
                for i in range(self.size["y"])
                for c in range(CORES)
            ]
        return lax.ppermute(value, "heads", pairs)

    def ring(self, value, way):
        held = [value]
        for _ in range(self.size[way] - 1):
            held.append(self.hop(held[-1], way))
        return held


def after(value, *others):
    return lax.optimization_barrier((value,) + others)[0]


def gather_blocks(place, stacked, order):
    first, second = order
    held = {}
    for i, a in enumerate(place.ring(stacked, first)):
        for j, b in enumerate(place.ring(a, second)):
            for k, c in enumerate(place.ring(b, "c")):
                held[(i, j, k) if first == "x" else (j, i, k)] = c
    return held


def owner(scalars, sizes, ways, steps):
    index = 0
    for way in ways:
        mine = scalars["xycz".index(way)]
        behind = lax.rem(mine + sizes[way] - steps[way], sizes[way])
        index = index * sizes[way] + behind
    return index


def ordered(place, value, dim, way):
    count = place.size[way]
    turned = jnp.flip(value, dim)
    return lax.dynamic_slice_in_dim(
        jnp.concatenate([turned, turned], dim), count - 1 - place.at[way], count, dim
    )


def assemble(place, held, row_ways, column_ways):
    sizes = place.size
    some = next(iter(held.values()))
    depth, r, c = some.shape
    keys = sorted(held)
    row_count = int(np.prod([sizes[w] for w in row_ways]))
    column_count = int(np.prod([sizes[w] for w in column_ways])) if column_ways else 1
    moves = [
        (n, kz, dict(x=kx, y=ky, c=kc, z=kz))
        for n, (kx, ky, kc) in enumerate(keys)
        for kz in range(depth)
    ]
    if r % 16:
        stacked = jnp.stack([held[k] for k in keys]).reshape(
            sizes["x"], sizes["y"], sizes["c"], depth, r, c
        )
        ways = list("xycz"[: 4 if depth > 1 else 3])
        if depth == 1:
            stacked = stacked[:, :, :, 0]
        for dim, way in enumerate(ways):
            stacked = ordered(place, stacked, dim, way)
        to = [ways.index(w) for w in row_ways] + [len(ways)]
        to += [ways.index(w) for w in column_ways] + [len(ways) + 1]
        return stacked.transpose(to).reshape(row_count * r, column_count * c)

    def body(scalars, *refs):
        ins, out, sems = refs[: len(keys)], refs[len(keys)], refs[len(keys) + 1]
        copies = []
        for at, (n, kz, steps) in enumerate(moves):
            row = pl.multiple_of(owner(scalars, sizes, row_ways, steps) * r, r)
            column = pl.multiple_of(owner(scalars, sizes, column_ways, steps) * c, c)
            copies.append(
                pltpu.make_async_copy(
                    ins[n].at[kz], out.at[pl.ds(row, r), pl.ds(column, c)], sems.at[at]
                )
            )
        for copy in copies:
            copy.start()
        for copy in copies:
            copy.wait()

    size = row_count * r * column_count * c * some.dtype.itemsize
    return pl.pallas_call(
        body,
        out_shape=jax.ShapeDtypeStruct((row_count * r, column_count * c), some.dtype),
        in_specs=[SMEM] + [ANY] * len(keys),
        out_specs=ANY,
        scratch_shapes=[pltpu.SemaphoreType.DMA((len(moves),))],
        cost_estimate=pl.CostEstimate(flops=0, bytes_accessed=2 * size, transcendentals=0),
    )(place.scalars, *[held[k] for k in keys])


def ring_sum(place, value, dim, way):
    count, mine = place.size[way], place.at[way]

    def pick(step):
        return lax.dynamic_index_in_dim(value, (mine + count - step) % count, dim, False)

    if count == 1:
        return pick(0)
    total = pick(1)
    for step in range(1, count):
        moved = place.hop(total.astype(jnp.bfloat16), way).astype(jnp.float32)
        total = moved + pick((step + 1) % count)
    return total


AXES = {"x": ("dp",), "yc": ("heads",), "z": ("tensor",)}


def axes_of(ways):
    names = []
    for part in ("x", "yc", "z"):
        if part in ways:
            names.append((ways.index(part), AXES[part][0]))
    return tuple(name for _, name in sorted(names))


def scatter_sum(place, value, ways, order):
    if not place.short:
        shape = value.shape[len(ways) :]
        for part in ("x", "yc", "z"):
            at = ways.find(part)
            if at >= 0:
                merged = value.shape[:at] + (-1,) + value.shape[at + len(part) :]
                value = lax.psum_scatter(
                    value.reshape(merged), AXES[part][0], scatter_dimension=at
                )
                ways = ways[:at] + ways[at + len(part) :]
        return value.reshape(shape)
    ways = list(ways)
    for way in order:
        dim = ways.index(way)
        value = ring_sum(place, value, dim, way)
        ways.pop(dim)
    return value


def relative_tables(grid_side):
    reach = 2 * grid_side - 1
    rows = np.arange(grid_side)
    delta = rows[:, None] - rows[None, :] + grid_side - 1
    one = (delta[:, :, None] == np.arange(reach)[None, None, :]).astype(np.float32)
    spread = np.einsum("rs,cmb->rbcsm", np.eye(grid_side, dtype=np.float32), one)
    side = grid_side * grid_side
    return one, spread.reshape(grid_side * reach, grid_side, side)


def bias_expand(table, grid_side):
    one, spread = relative_tables(grid_side)
    heads = table.shape[0]
    reach, side = 2 * grid_side - 1, grid_side * grid_side
    inner = table[:, : reach * reach].reshape(heads, reach, reach)
    rows = jnp.einsum("hab,rsa->hrsb", inner, one, precision=highest)
    rows = rows.reshape(heads * grid_side, grid_side * reach)
    full = jnp.einsum("nx,xck->nck", rows, spread, precision=highest)
    full = full.reshape(heads, side, side)
    corner = table[:, reach * reach :]
    left = jnp.broadcast_to(corner[:, 1][:, None, None], (heads, side, 1))
    top = jnp.concatenate(
        [corner[:, 2][:, None, None], jnp.broadcast_to(corner[:, 0][:, None, None], (heads, 1, side))],
        2,
    )
    return jnp.concatenate([top, jnp.concatenate([left, full], 2)], 1)


def bias_collect(grad, grid_side):
    one, spread = relative_tables(grid_side)
    heads = grad.shape[0]
    reach, side = 2 * grid_side - 1, grid_side * grid_side
    full = grad[:, 1:, 1:].reshape(heads * grid_side, grid_side, side)
    rows = jnp.einsum("nck,xck->nx", full, spread, precision=highest)
    rows = rows.reshape(heads, grid_side, grid_side, reach)
    inner = jnp.einsum("hrsb,rsa->hab", rows, one, precision=highest)
    return jnp.concatenate(
        [
            inner.reshape(heads, reach * reach),
            jnp.sum(grad[:, 0, 1:], -1, keepdims=True),
            jnp.sum(grad[:, 1:, 0], -1, keepdims=True),
            grad[:, 0, :1],
        ],
        1,
    )


def norm_rows(values, gain_row, shift_row):
    centred = values - jnp.mean(values, -1, keepdims=True)
    scaled = lax.rsqrt(jnp.mean(centred * centred, -1, keepdims=True) + epsilon)
    return centred * scaled * gain_row + shift_row


def contract_rows(left_side, right_side):
    return lax.dot_general(
        left_side, right_side, (((0,), (0,)), ((), ())), preferred_element_type=jnp.float32
    )


def contract_columns(left_side, right_side):
    return lax.dot_general(
        left_side, right_side, (((1,), (1,)), ((), ())), preferred_element_type=jnp.float32
    )


def split_columns(attention_full, groups):
    wide = attention_full.shape[1] // groups
    quarter = wide // 4
    blocks = attention_full.reshape(attention_full.shape[0], groups, wide)
    return (
        blocks[:, :, : 3 * quarter].reshape(attention_full.shape[0], -1),
        blocks[:, :, 3 * quarter :].reshape(attention_full.shape[0], -1),
    )


def attention_forward(normed, project_weight, output_weight, bias_grid, images, head_width):
    tokens = normed.shape[0] // images
    head_count = project_weight.shape[1] // (3 * head_width)
    projected = jnp.dot(normed, project_weight, preferred_element_type=jnp.float32).reshape(
        images, tokens, head_count, 3, head_width
    )
    query_rows = (projected[:, :, :, 0] * head_width ** (-0.5)).astype(jnp.bfloat16)
    key_rows = projected[:, :, :, 1].astype(jnp.bfloat16)
    value_rows = projected[:, :, :, 2].astype(jnp.bfloat16)
    scores = (
        jnp.einsum("gqhe,gkhe->ghqk", query_rows, key_rows, preferred_element_type=jnp.float32)
        + bias_grid[None]
    )
    score_max = jnp.max(scores, -1, keepdims=True)
    score_lse = jnp.log(jnp.sum(jnp.exp(scores - score_max), -1, keepdims=True)) + score_max
    weights = jnp.exp(scores - score_lse).astype(jnp.bfloat16)
    context = jnp.einsum(
        "ghqk,gkhe->gqhe", weights, value_rows, preferred_element_type=jnp.float32
    ).astype(jnp.bfloat16)
    context = context.reshape(images * tokens, head_count * head_width)
    return (
        contract_columns(context, output_weight),
        (query_rows, key_rows, value_rows, score_lse, context),
    )


def attention_backward(
    normed, attended_rows, project_weight, output_weight, saved, bias_grid, images, head_width, groups
):
    query_rows, key_rows, value_rows, score_lse, context = saved
    tokens = normed.shape[0] // images
    head_count = query_rows.shape[2]
    grad_context = jnp.dot(attended_rows, output_weight, preferred_element_type=jnp.float32).astype(
        jnp.bfloat16
    )
    grad_context = grad_context.reshape(images, tokens, head_count, head_width)
    scores = (
        jnp.einsum("gqhe,gkhe->ghqk", query_rows, key_rows, preferred_element_type=jnp.float32)
        + bias_grid[None]
    )
    weights = jnp.exp(scores - score_lse)
    grad_weights = jnp.einsum(
        "gqhe,gkhe->ghqk", grad_context, value_rows, preferred_element_type=jnp.float32
    )
    grad_value = jnp.einsum(
        "ghqk,gqhe->gkhe",
        weights.astype(jnp.bfloat16),
        grad_context,
        preferred_element_type=jnp.float32,
    )
    grad_scores = weights * (grad_weights - jnp.sum(weights * grad_weights, -1, keepdims=True))
    grad_bias = jnp.sum(grad_scores, 0)
    rounded = grad_scores.astype(jnp.bfloat16)
    grad_query = jnp.einsum(
        "ghqk,gkhe->gqhe", rounded, key_rows, preferred_element_type=jnp.float32
    ) * head_width ** (-0.5)
    grad_key = jnp.einsum(
        "ghqk,gqhe->gkhe", rounded, query_rows, preferred_element_type=jnp.float32
    )
    grad_projected = jnp.stack([grad_query, grad_key, grad_value], 3).astype(jnp.bfloat16)
    grad_projected = grad_projected.reshape(images * tokens, -1)
    by_group = grad_projected.reshape(images * tokens, groups, -1)
    context_groups = context.reshape(images * tokens, groups, -1)
    grad_project = jnp.stack(
        [contract_rows(normed, by_group[:, g]) for g in range(groups)]
    )
    grad_output = jnp.stack(
        [contract_rows(attended_rows, context_groups[:, g]) for g in range(groups)]
    )
    grad_attention = jnp.concatenate([grad_project, grad_output], 2)
    grad_normed = contract_columns(grad_projected, project_weight)
    return (grad_attention, grad_normed, grad_bias)


def adam_update(weight, first_moment, second_moment, gradient, rate):
    first_new = beta_one * first_moment + (1.0 - beta_one) * gradient
    second_new = beta_two * second_moment + (1.0 - beta_two) * gradient * gradient
    first_fix = 1.0 - beta_one**STEP
    second_fix = 1.0 - beta_two**STEP
    stepped = first_new / first_fix / (jnp.sqrt(second_new / second_fix) + adam_floor)
    return (weight - rate * (stepped + decay_rate * weight), first_new, second_new)


def shards(
    patches,
    masked,
    targets,
    patch_weight,
    patch_first,
    patch_second,
    attention_weight,
    attention_first,
    attention_second,
    hidden_weight,
    hidden_first,
    hidden_second,
    head_weight,
    head_first,
    head_second,
    vector_table,
    vector_first,
    vector_second,
    relative_bias,
    bias_first,
    bias_second,
):
    place = Place()
    sizes = place.size
    heads_index = lax.axis_index("heads")
    heads_size = lax.axis_size("heads")
    tensor_index = lax.axis_index("tensor")
    tensor_size = lax.axis_size("tensor")
    images = patches.shape[0] // heads_size
    patch_count = patches.shape[1]
    tokens = patch_count + 1
    marked = masked.shape[1]
    layer_count = attention_weight.shape[0]
    head_width = HEAD_DIM
    wide = patch_weight.shape[1]
    total_rows = patches.shape[0] * marked * lax.axis_size("dp") * tensor_size
    final_base = 6 * layer_count

    last = None
    gathered = []

    def fetch(shard, order, row_ways, column_ways):
        nonlocal last
        shard = shard.astype(jnp.bfloat16)
        if not place.short:
            full = lax.all_gather(shard, axes_of(row_ways), axis=0, tiled=True)
            if column_ways:
                full = lax.all_gather(full, axes_of(column_ways), axis=1, tiled=True)
            return full
        if last is not None:
            shard = after(shard, last)
        ring = place.ring(shard, "z")
        last = ring[-1]
        held = gather_blocks(place, jnp.stack(ring), order)
        return assemble(place, held, row_ways, column_ways)

    patch_full = fetch(patch_weight, "xy", "xycz", "")
    for layer_at in range(layer_count):
        attention_full = fetch(attention_weight[layer_at], "yx", "xz", "yc")
        up_full = fetch(hidden_weight[layer_at, 0], "xy", "xyc", "z")
        down_full = fetch(hidden_weight[layer_at, 1], "yx", "xyc", "z")
        gathered.append((split_columns(attention_full, heads_size), up_full, down_full))
    if place.short:
        head_held = gather_blocks(place, after(head_weight.astype(jnp.bfloat16), last)[None], "xy")
        head_full = assemble(place, head_held, "xyc", "")
    else:
        head_full = fetch(head_weight, "xy", "xyc", "")

    own = lambda a: lax.dynamic_slice_in_dim(a, heads_index * images, images)
    own_masked = own(masked)
    local_pixels = own(patches).reshape(images * patch_count, -1)
    embedded = jnp.dot(local_pixels, patch_full, preferred_element_type=jnp.float32)
    is_masked = jnp.any(own_masked[:, :, None] + 1 == jnp.arange(tokens)[None, None, :], axis=1)
    is_masked = is_masked[:, :, None]
    is_class = (jnp.arange(tokens) == 0)[None, :, None]
    residual = jnp.where(
        is_class,
        vector_table[final_base + 2],
        jnp.where(
            is_masked,
            vector_table[final_base + 3],
            jnp.pad(embedded.reshape(images, patch_count, wide), ((0, 0), (1, 0), (0, 0))),
        ),
    ).reshape(images * tokens, wide)
    bias_grid = bias_expand(relative_bias, GRID)

    saved_layers = []
    for layer_at in range(layer_count):
        (project_weight, output_weight), up_full, down_full = gathered[layer_at]
        gain_rows = vector_table[6 * layer_at : 6 * layer_at + 6]
        normed = norm_rows(residual, gain_rows[0], gain_rows[1]).astype(jnp.bfloat16)
        attended, saved_attention = attention_forward(
            normed, project_weight, output_weight, bias_grid, images, head_width
        )
        middle = residual + gain_rows[2] * attended
        mixed_rows = norm_rows(middle, gain_rows[3], gain_rows[4]).astype(jnp.bfloat16)
        hidden = jnp.dot(mixed_rows, up_full, preferred_element_type=jnp.float32)
        activated = jax.nn.gelu(hidden, approximate=False).astype(jnp.bfloat16)
        output = contract_columns(activated, down_full)
        saved_layers.append(
            (residual, middle, normed, saved_attention, attended, mixed_rows, hidden, activated, output)
        )
        residual = middle + gain_rows[5] * output
    final_rows = norm_rows(residual, vector_table[final_base], vector_table[final_base + 1]).astype(
        jnp.bfloat16
    )

    chosen = (jnp.arange(images)[:, None] * tokens + own_masked + 1).reshape(-1)
    share = chosen.shape[0]
    choose = (chosen[:, None] == jnp.arange(images * tokens)[None, :]).astype(jnp.bfloat16)
    picked = jnp.dot(choose, final_rows, preferred_element_type=jnp.float32).astype(jnp.bfloat16)
    head_rows = jnp.concatenate(place.ring(picked, "z"), 0)
    target_rows = targets.reshape(tensor_size, heads_size, share)
    target_rows = lax.dynamic_index_in_dim(target_rows, heads_index, 1, False)
    target_rows = ordered(place, target_rows, 0, "z").reshape(-1)
    logits = jnp.dot(head_rows, head_full, preferred_element_type=jnp.float32)
    block_width = logits.shape[1]
    onehot = jnp.arange(block_width)[None, :] + tensor_index * block_width == target_rows[:, None]
    local_max = jnp.max(logits, -1)
    local_sum = jnp.sum(jnp.exp(logits - local_max[:, None]), -1)
    local_pick = jnp.sum(jnp.where(onehot, logits, 0.0), -1)

    stats = jnp.stack([local_max, local_sum]).reshape(2, tensor_size, share)

    def turn(value, steps):
        count = tensor_size
        return lax.ppermute(value, "tensor", [(i, (i + steps) % count) for i in range(count)])

    every = [stats]
    for step in range(1, tensor_size):
        every.append(jnp.roll(turn(stats, step), step, 1))
    every = jnp.stack(every)
    score_max = jnp.max(every[:, 0], 0)
    score_sum = jnp.sum(every[:, 1] * jnp.exp(every[:, 0] - score_max), 0)
    log_total = (score_max + jnp.log(score_sum)).reshape(-1)
    loss_part = jnp.sum(log_total[:share]) - jnp.sum(local_pick)
    grad_logits = (
        (jnp.exp(logits - log_total[:, None]) - onehot.astype(jnp.float32)) / total_rows
    ).astype(jnp.bfloat16)
    grad_rows_all = contract_columns(grad_logits, head_full).reshape(tensor_size, share, wide)
    grad_picked = grad_rows_all[0]
    for step in range(1, tensor_size):
        grad_picked = grad_picked + turn(
            grad_rows_all[step].astype(jnp.bfloat16), tensor_size - step
        ).astype(jnp.float32)
    head_sum = contract_rows(head_rows, grad_logits)
    head_sum = head_sum.reshape(sizes["x"], sizes["y"], CORES, -1, block_width)
    head_grad = scatter_sum(place, head_sum, "xyc", "cxy")
    grad_final = lax.dot_general(
        choose.astype(jnp.float32), grad_picked, (((0,), (0,)), ((), ())), precision=highest
    )
    _, norm_back = jax.vjp(
        norm_rows, residual, vector_table[final_base], vector_table[final_base + 1]
    )
    grad_residual, grad_final_gain, grad_final_shift = norm_back(grad_final)

    bias_grad = jnp.zeros(bias_grid.shape, jnp.float32)
    layer_grads = [None] * layer_count
    attention_grads = [None] * layer_count
    hidden_grads = [None] * layer_count
    hidden_view = (tensor_size, sizes["x"], sizes["y"], CORES, -1, hidden_weight.shape[-1])
    attention_view = (sizes["y"], CORES, sizes["x"], tensor_size, -1, attention_weight.shape[-1])

    def by_tensor(left_side, right_side):
        pieces = right_side.reshape(right_side.shape[0], tensor_size, -1)
        return jnp.stack([contract_rows(left_side, pieces[:, t]) for t in range(tensor_size)])

    for layer_at in reversed(range(layer_count)):
        residual_in, middle, normed, saved_attention, attended, mixed_rows, hidden, activated, output = (
            saved_layers[layer_at]
        )
        (project_weight, output_weight), up_full, down_full = gathered[layer_at]
        gain_rows = vector_table[6 * layer_at : 6 * layer_at + 6]
        grad_rows = [None] * 6
        grad_rows[5] = jnp.sum(grad_residual * output, 0)
        grad_output = (grad_residual * gain_rows[5]).astype(jnp.bfloat16)
        grad_activated = jnp.dot(grad_output, down_full, preferred_element_type=jnp.float32)
        grad_down = by_tensor(grad_output, activated)
        _, gelu_back = jax.vjp(partial(jax.nn.gelu, approximate=False), hidden)
        grad_hidden = gelu_back(grad_activated)[0].astype(jnp.bfloat16)
        grad_up = by_tensor(mixed_rows, grad_hidden)
        hidden_grads[layer_at] = jnp.stack(
            [
                scatter_sum(place, grad_up.reshape(hidden_view), "zxyc", "cxyz"),
                scatter_sum(place, grad_down.reshape(hidden_view), "zxyc", "cyxz"),
            ]
        )
        grad_mixed = contract_columns(grad_hidden, up_full)
        _, norm_back = jax.vjp(norm_rows, middle, gain_rows[3], gain_rows[4])
        grad_middle, grad_rows[3], grad_rows[4] = norm_back(grad_mixed)
        grad_middle = grad_middle + grad_residual
        grad_rows[2] = jnp.sum(grad_middle * attended, 0)
        grad_attended = (grad_middle * gain_rows[2]).astype(jnp.bfloat16)
        grad_attention, grad_normed, grad_bias = attention_backward(
            normed,
            grad_attended,
            project_weight,
            output_weight,
            saved_attention,
            bias_grid,
            images,
            head_width,
            heads_size,
        )
        attention_grads[layer_at] = scatter_sum(
            place, grad_attention.reshape(attention_view), "ycxz", "cxyz"
        )
        _, norm_back = jax.vjp(norm_rows, residual_in, gain_rows[0], gain_rows[1])
        grad_input, grad_rows[0], grad_rows[1] = norm_back(grad_normed)
        grad_residual = grad_input + grad_middle
        bias_grad = bias_grad + grad_bias
        layer_grads[layer_at] = jnp.stack(grad_rows)
    grad_residual = grad_residual.reshape(images, tokens, wide)
    grad_embedded = jnp.where(is_masked, 0.0, grad_residual)[:, 1:].astype(jnp.bfloat16)
    patch_sum = contract_rows(local_pixels, grad_embedded.reshape(images * patch_count, wide))
    patch_view = (sizes["x"], sizes["y"], CORES, tensor_size, -1, wide)
    patch_grad = scatter_sum(place, patch_sum.reshape(patch_view), "xycz", "cxyz")
    grad_class = jnp.sum(grad_residual[:, 0], 0)
    grad_mask = jnp.sum(jnp.where(is_masked, grad_residual, 0.0), (0, 1))
    vector_grad = jnp.concatenate(
        layer_grads + [jnp.stack([grad_final_gain, grad_final_shift, grad_class, grad_mask])], 0
    )
    relative_grad = bias_collect(bias_grad, GRID)

    sizes_flat = (1, vector_grad.size, relative_grad.size)
    flat = jnp.concatenate([loss_part.reshape(1), vector_grad.reshape(-1), relative_grad.reshape(-1)])
    flat = jnp.pad(flat, (0, -flat.size % 1024)).reshape(-1, 128)
    for way in "cxyz":
        flat = sum(place.ring(flat, way)[1:], flat) if sizes[way] <= 2 else ring_total(place, flat, way)
    flat = flat.reshape(-1)
    loss = flat[0] / total_rows
    vector_grad = flat[1 : 1 + sizes_flat[1]].reshape(vector_grad.shape)
    relative_grad = flat[1 + sizes_flat[1] : sum(sizes_flat)].reshape(relative_grad.shape)

    params = (patch_weight, attention_weight, hidden_weight, head_weight, vector_table, relative_bias)
    firsts = (patch_first, attention_first, hidden_first, head_first, vector_first, bias_first)
    seconds = (patch_second, attention_second, hidden_second, head_second, vector_second, bias_second)
    gradients = (
        patch_grad,
        jnp.stack(attention_grads),
        jnp.stack(hidden_grads),
        head_grad,
        vector_grad,
        relative_grad,
    )
    results = [loss]
    for member in range(6):
        results.extend(
            adam_update(
                params[member], firsts[member], seconds[member], gradients[member], learning_rates[member]
            )
        )
    return tuple(results)


def ring_total(place, value, way):
    held = jnp.stack(place.ring(value, way))
    count = place.size[way]
    canonical = (place.at[way] + count - jnp.arange(count)) % count
    total = None
    for entry in range(count):
        part = lax.dynamic_index_in_dim(held, canonical[entry], 0, False)
        total = part if total is None else total + part
    return total


def solution(mesh):
    rows_all = P(("dp", "heads", "tensor"), None)
    attention = P(None, ("dp", "tensor"), "heads")
    hidden = P(None, None, ("dp", "heads"), "tensor")
    head = P(("dp", "heads"), "tensor")
    states = (rows_all,) * 3 + (attention,) * 3 + (hidden,) * 3 + (head,) * 3 + (P(),) * 6
    return jax.shard_map(
        shards,
        mesh=mesh,
        in_specs=(P(("dp", "tensor"), None, None), P(("dp", "tensor"), None), P("dp", None)) + states,
        out_specs=(P(),) + states,
        check_vma=False,
    )
```

time: 1780 us -> 2010 us (1.13)
  Pallas kernels: 0 us -> 967 us
  blocking collectives: 441 us -> 0 us
  waiting for transfers between devices: 507 us -> 255 us
  other arithmetic: 292 us -> 145 us
  starting transfers between devices: 17.3 us -> 88.6 us
  matrix products: 170 us -> 241 us
  local copies, waits for them, and re-layouts: 315 us -> 289 us
    pallas_call x0 -> x7, Pallas kernels: none -> 967 us  [assemble(): pl.pallas_call(body, out_shape=jax.ShapeDtypeStruct((row_count * r, colum...]
    all_gather x15 -> x0, waiting for transfers between devices: 451 us -> none  [the longest x4 217 us: rows_tensor(): return lax.all_gather(values, 'tensor', axis=0, tiled=True)]
    unnamed x11 -> x0, blocking collectives: 375 us -> none
    ppermute x0 -> x137, waiting for transfers between devices: none -> 255 us  [the longest x69 246 us: hop(): lax.ppermute(value, axis, [(i, (i + 1) % count) for i in range(count)])]
    scatter-add x2 -> x0, other arithmetic: 212 us -> none  [the longest x1 208 us: shards(): jax.ops.segment_sum(bias_grad.reshape(head_count, -1).T, index_table.resh...]
    gather x5 -> x0, local copies, waits for them, and re-layouts: 144 us -> none  [the longest x4 140 us: shards(): bias_grid = jnp.take(own_bias, index_table, axis=1)]
    ppermute x0 -> x137, starting transfers between devices: none -> 88.6 us  [the longest x69 52.6 us: hop(): lax.ppermute(value, axis, [(i, (i + 1) % count) for i in range(count)])]
    unnamed x340 -> x418, local copies, waits for them, and re-layouts: 105 us -> 47.6 us
  transfers between devices with their start and end apart: 31 -> 137, of which waited for: 23 -> 48; matrix products, arithmetic and copies ran while one was open for 30% -> 30% of each run, Pallas kernels for 0% -> 48%
where the time goes in v1:
time: 2010 us; the launch traced here: 2000 us
  Pallas kernels  967 us (48%)
  local copies, waits for them, and re-layouts  289 us (14%)
  waiting for transfers between devices  255 us (13%)
  matrix products  241 us (12%)
  other arithmetic  145 us (7%)
  starting transfers between devices  88.6 us (4%)
    pallas_call x7, Pallas kernels, assemble(): pl.pallas_call(body, out_shape=jax.ShapeDtypeStruct((row_count * r, colum...  967 us
    ppermute x69, waiting for transfers between devices, hop(): lax.ppermute(value, axis, [(i, (i + 1) % count) for i in range(count)])  246 us
    dot_general x34, matrix products, contract_rows(): lax.dot_general(left_side, right_side, (((0,), (0,)), ((), ())), preferre...  70.2 us
    ppermute x69, starting transfers between devices, hop(): lax.ppermute(value, axis, [(i, (i + 1) % count) for i in range(count)])  52.6 us
    unnamed x418, local copies, waits for them, and re-layouts  47.6 us
  transfers between devices with their start and end apart: 137, of which 48 were waited for; matrix products, arithmetic and copies ran while one was open for 30% of the time, Pallas kernels for 48%

profile of v1, /device:TPU:0, one launch (start us, length us, event | category | flops | bytes accessed | tf_op | source)
XLA Modules:
  0.0 2001.8 jit_solution(17364821013213514385)
XLA Ops:
  175.2 145.0 %shard_map.384 = bf16[768,3072]{1,0:T(8,128)(2,1)} custom-call(s32[4]{0:T(128)} %pad_add_fusion.scalars, bf16[4,96,768]{2,1,0:T(8,128)(2,1)} %pad_maximum_fusion.6.refs_0_, bf16[4,96,768]{2,1,0:T(8,128)(2,1)} %collective-permute-done.13.refs_1_, bf16[4,96,768]{2,1,0:T(8,128)(2,1)} %collective-permute-done.14.refs_2_, ...), custom_call_target="tpu_custom_call" | custom-call | bytes 9437184 | tf_op jit(solution)/shard_map/pallas_call | solution.py:145
  355.0 145.1 %shard_map.385 = bf16[768,3072]{1,0:T(8,128)(2,1)} custom-call(s32[4]{0:T(128)} %pad_add_fusion.scalars, bf16[4,96,768]{2,1,0:T(8,128)(2,1)} %pad_maximum_fusion.7.refs_0_, bf16[4,96,768]{2,1,0:T(8,128)(2,1)} %collective-permute-done.23.refs_1_, bf16[4,96,768]{2,1,0:T(8,128)(2,1)} %collective-permute-done.24.refs_2_, ...), custom_call_target="tpu_custom_call" | custom-call | bytes 9437184 | tf_op jit(solution)/shard_map/pallas_call | solution.py:145
  502.8 16.1 multiply_convert_fusion.1
  529.7 145.0 %shard_map.386 = bf16[768,3072]{1,0:T(8,128)(2,1)} custom-call(s32[4]{0:T(128)} %pad_add_fusion.scalars, bf16[4,96,768]{2,1,0:T(8,128)(2,1)} %pad_maximum_fusion.8.refs_0_, bf16[4,96,768]{2,1,0:T(8,128)(2,1)} %copy-done.108, bf16[4,96,768]{2,1,0:T(8,128)(2,1)} %collective-permute-done.34.refs_2_, bf16[4,96,768]{2,1,0:T(8,128)(2,1)} %collective-permute-done.35.refs_3_, ...), custom_call_target="tpu_custom_call" | custom-call | bytes 9437184 | tf_op jit(solution)/shard_map/pallas_call | solution.py:145
  686.7 145.0 %shard_map.387 = bf16[768,3072]{1,0:T(8,128)(2,1)} custom-call(s32[4]{0:T(128)} %pad_add_fusion.scalars, bf16[4,96,768]{2,1,0:T(8,128)(2,1)} %pad_maximum_fusion.9.refs_0_, bf16[4,96,768]{2,1,0:T(8,128)(2,1)} %collective-permute-done.43.refs_1_, bf16[4,96,768]{2,1,0:T(8,128)(2,1)} %collective-permute-done.44.refs_2_, ...), custom_call_target="tpu_custom_call" | custom-call | bytes 9437184 | tf_op jit(solution)/shard_map/pallas_call | solution.py:145
  864.2 12.1 collective-permute-done.68.refs_6_
  877.6 145.0 %shard_map.388 = bf16[768,3072]{1,0:T(8,128)(2,1)} custom-call(s32[4]{0:T(128)} %pad_add_fusion.scalars, bf16[4,96,768]{2,1,0:T(8,128)(2,1)} %pad_maximum_fusion.10.refs_0_, bf16[4,96,768]{2,1,0:T(8,128)(2,1)} %collective-permute-done.53.refs_1_, bf16[4,96,768]{2,1,0:T(8,128)(2,1)} %collective-permute-done.54.refs_2_, bf16[4,96,768]{2,1,0:T(8,128)(2,1)} %copy-done.111, ...), custom_call_target="tpu_custom_call" | custom-call | bytes 9437184 | tf_op jit(solution)/shard_map/pallas_call | solution.py:145
  1022.7 16.4 multiply_convert_fusion
  1039.1 145.0 %shard_map.389 = bf16[768,3072]{1,0:T(8,128)(2,1)} custom-call(s32[4]{0:T(128)} %pad_add_fusion.scalars, bf16[4,96,768]{2,1,0:T(8,128)(2,1)} %pad_maximum_fusion.11.refs_0_, bf16[4,96,768]{2,1,0:T(8,128)(2,1)} %collective-permute-done.63.refs_1_, bf16[4,96,768]{2,1,0:T(8,128)(2,1)} %collective-permute-done.64.refs_2_, ...), custom_call_target="tpu_custom_call" | custom-call | bytes 9437184 | tf_op jit(solution)/shard_map/pallas_call | solution.py:145
  1223.5 9.8 fusion.174
  1236.5 97.1 %shard_map.390 = bf16[768,2048]{1,0:T(8,128)(2,1)} custom-call(s32[4]{0:T(128)} %pad_add_fusion.scalars, bf16[1,96,2048]{2,1,0:T(8,128)(2,1)} %bitcast.73.refs_0_, bf16[1,96,2048]{2,1,0:T(8,128)(2,1)} %collective-permute-done.73.refs_1_, bf16[1,96,2048]{2,1,0:T(8,128)(2,1)} %collective-permute-done.74.refs_2_, ...), custom_call_target="tpu_custom_call" | custom-call | bytes 6291456 | tf_op jit(solution)/shard_map/pallas_call | solution.py:145
  1354.9 8.9 fusion.176
  1399.6 8.0 add_convert_fusion.1
  1460.7 8.1 add_convert_fusion
  1577.2 20.5 %convolution_bitcast_fusion.24 = f32[12,14,14,27]{3,0,2,1:T(8,128)S(1)} fusion(f32[12,14,14,196,1]{3,0,2,4,1:T(8,128)} %bitcast.836, f32[14,27,14,196,1]{3,1,2,0,4:T(8,128)} %constant.615), kind=kOutput, calls=%fused_computation.142 | convolution fusion | flops 2091059712 | bytes 6246912 | tf_op jit(solution)/shard_map/nck,xck->nx/dot_general | solution.py:234
  1618.1 9.6 copy.448
  1638.1 9.6 copy.441
  1673.0 8.2 fusion.175
  1791.1 8.5 collective-permute-done.135
  1847.7 21.8 %collective-permute-done.99 = bf16[2,4,96,768]{3,2,1,0:T(8,128)(2,1)} collective-permute-done((bf16[2,4,96,768]{3,2,1,0:T(8,128)(2,1)S(1)}, bf16[2,4,96,768]{3,2,1,0:T(8,128)(2,1)}, u32[]{:S(2)}, u32[]{:S(2)}) %collective-permute-start.99) | collective-permute-done | bytes 1179680 | tf_op jit(solution)/shard_map/ppermute | solution.py:50
  1875.5 19.4 collective-permute-done.123
  1900.0 20.0 collective-permute-done.111
  1923.9 8.7 collective-permute-done.130
  1933.8 10.6 collective-permute-done.118
  (1061 shorter events, 803.0 us)
Async XLA Ops:
  172.5 164.0 %collective-permute-start.23 = (bf16[4,96,768]{2,1,0:T(8,128)(2,1)}, bf16[4,96,768]{2,1,0:T(8,128)(2,1)}, u32[]{:S(2)}, u32[]{:S(2)}) collective-permute-start(bf16[4,96,768]{2,1,0:T(8,128)(2,1)} %pad_maximum_fusion.7.refs_0_), channel_id=1, source_target_pairs={{0,4},{4,0},{8,12},{12,8},{1,5},{5,1},{9,13},{13,9},{2,6},{6,2},{1... | collective-permute-start | bytes 1769480 | tf_op jit(solution)/shard_map/ppermute | solution.py:63
  173.0 175.6 %collective-permute-start.34 = (bf16[4,96,768]{2,1,0:T(8,128)(2,1)}, bf16[4,96,768]{2,1,0:T(8,128)(2,1)}, u32[]{:S(2)}, u32[]{:S(2)}) collective-permute-start(bf16[4,96,768]{2,1,0:T(8,128)(2,1)} %pad_maximum_fusion.8.refs_0_), channel_id=1, source_target_pairs={{0,8},{4,12},{8,0},{12,4},{1,9},{5,13},{9,1},{13,5},{2,10},{6,14},... | collective-permute-start | bytes 1769480 | tf_op jit(solution)/shard_map/ppermute | solution.py:63
  173.0 177.1 %collective-permute-start.27 = (bf16[4,96,768]{2,1,0:T(8,128)(2,1)}, bf16[4,96,768]{2,1,0:T(8,128)(2,1)}, u32[]{:S(2)}, u32[]{:S(2)}) collective-permute-start(bf16[4,96,768]{2,1,0:T(8,128)(2,1)} %collective-permute-done.26.refs_4_), channel_id=1, source_target_pairs={{0,4},{4,0},{8,12},{12,8},{1,5},{5,1},{9,13},{13,9},{2,6},{6,2},{1... | collective-permute-start | bytes 1769480 | tf_op jit(solution)/shard_map/ppermute | solution.py:63
  173.1 168.8 %collective-permute-start.28 = (bf16[4,96,768]{2,1,0:T(8,128)(2,1)}, bf16[4,96,768]{2,1,0:T(8,128)(2,1)}, u32[]{:S(2)}, u32[]{:S(2)}) collective-permute-start(bf16[4,96,768]{2,1,0:T(8,128)(2,1)} %collective-permute-done.26.refs_4_), channel_id=1, source_target_pairs={{0,8},{4,12},{8,0},{12,4},{1,9},{5,13},{9,1},{13,5},{2,10},{6,14},... | collective-permute-start | bytes 1769480 | tf_op jit(solution)/shard_map/ppermute | solution.py:63
  175.1 173.6 %collective-permute-start.25 = (bf16[4,96,768]{2,1,0:T(8,128)(2,1)}, bf16[4,96,768]{2,1,0:T(8,128)(2,1)}, u32[]{:S(2)}, u32[]{:S(2)}) collective-permute-start(bf16[4,96,768]{2,1,0:T(8,128)(2,1)} %collective-permute-done.24.refs_2_), channel_id=1, source_target_pairs={{0,4},{4,0},{8,12},{12,8},{1,5},{5,1},{9,13},{13,9},{2,6},{6,2},{1... | collective-permute-start | bytes 1769480 | tf_op jit(solution)/shard_map/ppermute | solution.py:63
  348.7 152.2 %collective-permute-start.36 = (bf16[4,96,768]{2,1,0:T(8,128)(2,1)}, bf16[4,96,768]{2,1,0:T(8,128)(2,1)}, u32[]{:S(2)}, u32[]{:S(2)}) collective-permute-start(bf16[4,96,768]{2,1,0:T(8,128)(2,1)} %pad_maximum_fusion.8.refs_0_), channel_id=1, source_target_pairs={{0,16},{16,0},{1,17},{17,1},{2,18},{18,2},{3,19},{19,3},{4,20},{20... | collective-permute-start | bytes 1769480 | tf_op jit(solution)/shard_map/ppermute | solution.py:50
  520.8 162.8 %collective-permute-start.43 = (bf16[4,96,768]{2,1,0:T(8,128)(2,1)}, bf16[4,96,768]{2,1,0:T(8,128)(2,1)}, u32[]{:S(2)}, u32[]{:S(2)}) collective-permute-start(bf16[4,96,768]{2,1,0:T(8,128)(2,1)} %pad_maximum_fusion.9.refs_0_), channel_id=1, source_target_pairs={{0,4},{4,0},{8,12},{12,8},{1,5},{5,1},{9,13},{13,9},{2,6},{6,2},{1... | collective-permute-start | bytes 1769480 | tf_op jit(solution)/shard_map/ppermute | solution.py:63
  521.3 162.3 %collective-permute-start.56 = (bf16[4,96,768]{2,1,0:T(8,128)(2,1)}, bf16[4,96,768]{2,1,0:T(8,128)(2,1)}, u32[]{:S(2)}, u32[]{:S(2)}) collective-permute-start(bf16[4,96,768]{2,1,0:T(8,128)(2,1)} %pad_maximum_fusion.10.refs_0_), channel_id=1, source_target_pairs={{0,16},{16,0},{1,17},{17,1},{2,18},{18,2},{3,19},{19,3},{4,20},{20... | collective-permute-start | bytes 1769480 | tf_op jit(solution)/shard_map/ppermute | solution.py:50
  522.0 162.4 %collective-permute-start.45 = (bf16[4,96,768]{2,1,0:T(8,128)(2,1)}, bf16[4,96,768]{2,1,0:T(8,128)(2,1)}, u32[]{:S(2)}, u32[]{:S(2)}) collective-permute-start(bf16[4,96,768]{2,1,0:T(8,128)(2,1)} %collective-permute-done.44.refs_2_), channel_id=1, source_target_pairs={{0,4},{4,0},{8,12},{12,8},{1,5},{5,1},{9,13},{13,9},{2,6},{6,2},{1... | collective-permute-start | bytes 1769480 | tf_op jit(solution)/shard_map/ppermute | solution.py:63
  529.1 156.5 %collective-permute-start.47 = (bf16[4,96,768]{2,1,0:T(8,128)(2,1)}, bf16[4,96,768]{2,1,0:T(8,128)(2,1)}, u32[]{:S(2)}, u32[]{:S(2)}) collective-permute-start(bf16[4,96,768]{2,1,0:T(8,128)(2,1)} %collective-permute-done.46.refs_4_), channel_id=1, source_target_pairs={{0,4},{4,0},{8,12},{12,8},{1,5},{5,1},{9,13},{13,9},{2,6},{6,2},{1... | collective-permute-start | bytes 1769480 | tf_op jit(solution)/shard_map/ppermute | solution.py:63
  529.2 157.2 %collective-permute-start.49 = (bf16[4,96,768]{2,1,0:T(8,128)(2,1)}, bf16[4,96,768]{2,1,0:T(8,128)(2,1)}, u32[]{:S(2)}, u32[]{:S(2)}) collective-permute-start(bf16[4,96,768]{2,1,0:T(8,128)(2,1)} %collective-permute-done.48.refs_6_), channel_id=1, source_target_pairs={{0,4},{4,0},{8,12},{12,8},{1,5},{5,1},{9,13},{13,9},{2,6},{6,2},{1... | collective-permute-start | bytes 1769480 | tf_op jit(solution)/shard_map/ppermute | solution.py:63
  683.6 175.7 %collective-permute-start.53 = (bf16[4,96,768]{2,1,0:T(8,128)(2,1)}, bf16[4,96,768]{2,1,0:T(8,128)(2,1)}, u32[]{:S(2)}, u32[]{:S(2)}) collective-permute-start(bf16[4,96,768]{2,1,0:T(8,128)(2,1)} %pad_maximum_fusion.10.refs_0_), channel_id=1, source_target_pairs={{0,4},{4,0},{8,12},{12,8},{1,5},{5,1},{9,13},{13,9},{2,6},{6,2},{1... | collective-permute-start | bytes 1769480 | tf_op jit(solution)/shard_map/ppermute | solution.py:63
  683.6 175.8 %collective-permute-start.54 = (bf16[4,96,768]{2,1,0:T(8,128)(2,1)}, bf16[4,96,768]{2,1,0:T(8,128)(2,1)}, u32[]{:S(2)}, u32[]{:S(2)}) collective-permute-start(bf16[4,96,768]{2,1,0:T(8,128)(2,1)} %pad_maximum_fusion.10.refs_0_), channel_id=1, source_target_pairs={{0,8},{4,12},{8,0},{12,4},{1,9},{5,13},{9,1},{13,5},{2,10},{6,14},... | collective-permute-start | bytes 1769480 | tf_op jit(solution)/shard_map/ppermute | solution.py:63
  684.4 175.5 %collective-permute-start.64 = (bf16[4,96,768]{2,1,0:T(8,128)(2,1)}, bf16[4,96,768]{2,1,0:T(8,128)(2,1)}, u32[]{:S(2)}, u32[]{:S(2)}) collective-permute-start(bf16[4,96,768]{2,1,0:T(8,128)(2,1)} %pad_maximum_fusion.11.refs_0_), channel_id=1, source_target_pairs={{0,8},{4,12},{8,0},{12,4},{1,9},{5,13},{9,1},{13,5},{2,10},{6,14},... | collective-permute-start | bytes 1769480 | tf_op jit(solution)/shard_map/ppermute | solution.py:63
  685.7 176.2 %collective-permute-start.66 = (bf16[4,96,768]{2,1,0:T(8,128)(2,1)}, bf16[4,96,768]{2,1,0:T(8,128)(2,1)}, u32[]{:S(2)}, u32[]{:S(2)}) collective-permute-start(bf16[4,96,768]{2,1,0:T(8,128)(2,1)} %pad_maximum_fusion.11.refs_0_), channel_id=1, source_target_pairs={{0,16},{16,0},{1,17},{17,1},{2,18},{18,2},{3,19},{19,3},{4,20},{20... | collective-permute-start | bytes 1769480 | tf_op jit(solution)/shard_map/ppermute | solution.py:50
  686.4 175.2 %collective-permute-start.58 = (bf16[4,96,768]{2,1,0:T(8,128)(2,1)}, bf16[4,96,768]{2,1,0:T(8,128)(2,1)}, u32[]{:S(2)}, u32[]{:S(2)}) collective-permute-start(bf16[4,96,768]{2,1,0:T(8,128)(2,1)} %collective-permute-done.56.refs_4_), channel_id=1, source_target_pairs={{0,8},{4,12},{8,0},{12,4},{1,9},{5,13},{9,1},{13,5},{2,10},{6,14},... | collective-permute-start | bytes 1769480 | tf_op jit(solution)/shard_map/ppermute | solution.py:63
  861.9 177.1 %collective-permute-start.63 = (bf16[4,96,768]{2,1,0:T(8,128)(2,1)}, bf16[4,96,768]{2,1,0:T(8,128)(2,1)}, u32[]{:S(2)}, u32[]{:S(2)}) collective-permute-start(bf16[4,96,768]{2,1,0:T(8,128)(2,1)} %pad_maximum_fusion.11.refs_0_), channel_id=1, source_target_pairs={{0,4},{4,0},{8,12},{12,8},{1,5},{5,1},{9,13},{13,9},{2,6},{6,2},{1... | collective-permute-start | bytes 1769480 | tf_op jit(solution)/shard_map/ppermute | solution.py:63
  862.5 332.5 %collective-permute-start.76 = (bf16[1,96,2048]{2,1,0:T(8,128)(2,1)}, bf16[1,96,2048]{2,1,0:T(8,128)(2,1)}, u32[]{:S(2)}, u32[]{:S(2)}) collective-permute-start(bf16[1,96,2048]{2,1,0:T(8,128)(2,1)} %bitcast.73.refs_0_), channel_id=1, source_target_pairs={{0,16},{16,0},{1,17},{17,1},{2,18},{18,2},{3,19},{19,3},{4,20},{20... | collective-permute-start | bytes 1179656 | tf_op jit(solution)/shard_map/ppermute | solution.py:50
  864.2 174.9 %collective-permute-start.65 = (bf16[4,96,768]{2,1,0:T(8,128)(2,1)}, bf16[4,96,768]{2,1,0:T(8,128)(2,1)}, u32[]{:S(2)}, u32[]{:S(2)}) collective-permute-start(bf16[4,96,768]{2,1,0:T(8,128)(2,1)} %collective-permute-done.64.refs_2_), channel_id=1, source_target_pairs={{0,4},{4,0},{8,12},{12,8},{1,5},{5,1},{9,13},{13,9},{2,6},{6,2},{1... | collective-permute-start | bytes 1769480 | tf_op jit(solution)/shard_map/ppermute | solution.py:63
  876.3 162.8 %collective-permute-start.67 = (bf16[4,96,768]{2,1,0:T(8,128)(2,1)}, bf16[4,96,768]{2,1,0:T(8,128)(2,1)}, u32[]{:S(2)}, u32[]{:S(2)}) collective-permute-start(bf16[4,96,768]{2,1,0:T(8,128)(2,1)} %collective-permute-done.66.refs_4_), channel_id=1, source_target_pairs={{0,4},{4,0},{8,12},{12,8},{1,5},{5,1},{9,13},{13,9},{2,6},{6,2},{1... | collective-permute-start | bytes 1769480 | tf_op jit(solution)/shard_map/ppermute | solution.py:63
  877.2 161.9 %collective-permute-start.69 = (bf16[4,96,768]{2,1,0:T(8,128)(2,1)S(1)}, bf16[4,96,768]{2,1,0:T(8,128)(2,1)}, u32[]{:S(2)}, u32[]{:S(2)}) collective-permute-start(bf16[4,96,768]{2,1,0:T(8,128)(2,1)S(1)} %collective-permute-done.68.refs_6_), channel_id=1, source_target_pairs={{0,4},{4,0},{8,12},{12,8},{1,5},{5,1},{9,13},{13,9},{2,6},{6,2},{1... | collective-permute-start | bytes 1769480 | tf_op jit(solution)/shard_map/ppermute | solution.py:63
  1389.8 386.2 %collective-permute-start.134 = (bf16[2,2,96,2048]{3,2,1,0:T(8,128)(2,1)}, bf16[2,2,96,2048]{3,2,1,0:T(8,128)(2,1)}, u32[]{:S(2)}, u32[]{:S(2)}) collective-permute-start(bf16[2,2,96,2048]{3,2,1,0:T(8,128)(2,1)} %fusion.24), channel_id=1, source_target_pairs={{0,4},{4,0},{8,12},{12,8},{1,5},{5,1},{9,13},{13,9},{2,6},{6,2},{1... | collective-permute-start | bytes 4718600 | tf_op jit(solution)/shard_map/ppermute | solution.py:63
  1632.0 170.1 %collective-permute-start.104 = (bf16[2,2,4,96,768]{4,3,2,0,1:T(8,128)(2,1)}, bf16[2,2,4,96,768]{4,3,2,0,1:T(8,128)(2,1)}, u32[]{:S(2)}, u32[]{:S(2)}) collective-permute-start(bf16[2,2,4,96,768]{4,3,2,0,1:T(8,128)(2,1)} %fusion.23), channel_id=1, source_target_pairs={{0,4},{4,0},{8,12},{12,8},{1,5},{5,1},{9,13},{13,9},{2,6},{6,2},{1... | collective-permute-start | bytes 7077896 | tf_op jit(solution)/shard_map/ppermute | solution.py:63
  1651.8 158.1 %collective-permute-start.98 = (bf16[2,2,4,96,768]{4,3,2,1,0:T(8,128)(2,1)}, bf16[2,2,4,96,768]{4,3,2,1,0:T(8,128)(2,1)}, u32[]{:S(2)}, u32[]{:S(2)}) collective-permute-start(bf16[2,2,4,96,768]{4,3,2,1,0:T(8,128)(2,1)} %fusion.18), channel_id=1, source_target_pairs={{0,4},{4,0},{8,12},{12,8},{1,5},{5,1},{9,13},{13,9},{2,6},{6,2},{1... | collective-permute-start | bytes 7077896 | tf_op jit(solution)/shard_map/ppermute | solution.py:63
  (317 other events, 7187.0 us)
